TPU v7x, 256 devices: a whole 4x4x8 slice. The times are simulated.
256 devices in a mesh: row: 64 (over y, x_hi, z), ch: 4 (over x_lo, core).
Axes of the slice: x: 4 (x_hi: 2, x_lo: 2; x = x_hi * 2 + x_lo), y: 4, z: 8, core: 2. Of those that a mesh axis runs over, the one named last changes fastest.
Arguments:
- pair_field: bfloat16 [128, 512, 512], P('ch', 'row'), may hold values from -25 to 25
- input_gain: float32 [128], replicated, may hold values from 0.5 to 1.5
- input_bias: float32 [128], replicated, may hold values from -1.2 to 1.2
- left_weight: bfloat16 [128, 128], P(None, 'ch'), may hold values from -0.5 to 0.5
- left_gate: bfloat16 [128, 128], P(None, 'ch'), may hold values from -0.5 to 0.5
- right_weight: bfloat16 [128, 128], P(None, 'ch'), may hold values from -0.5 to 0.5
- right_gate: bfloat16 [128, 128], P(None, 'ch'), may hold values from -0.5 to 0.5
- gate_weight: bfloat16 [128, 128], P(None, 'ch'), may hold values from -0.5 to 0.5
- output_gain: float32 [128], replicated, may hold values from 0.5 to 1.5
- output_bias: float32 [128], replicated, may hold values from -1.2 to 1.2
- final_weight: bfloat16 [128, 128], P(None, 'ch'), may hold values from -0.5 to 0.5
Outputs:
- transposed: bfloat16 [128, 512, 512], P('ch', 'row')
All inputs are finite; a program needn't handle non-finite values.
Results may differ from a plain program's by a relative error of at most 0.012.
Values may be sent and summed in bfloat16 or wider, within the bound.
No kernel may reach another device: no remote copies, remote signals or barrier semaphores. Data moves between devices by JAX's collectives and lax.ppermute only.
A program may use at most 64 MiB of HBM per device.

v0:
```python
import jax
import jax.numpy as jnp
from jax import lax
from jax.sharding import PartitionSpec as P

epsilon = 1e-05


def layer_norm(values, gain, bias):
    average = jnp.mean(values, axis=0, keepdims=True)
    centred = values - average
    variance = jnp.mean(centred * centred, axis=0, keepdims=True)
    return centred * lax.rsqrt(variance + epsilon) * gain[:, None, None] + bias[:, None, None]


def project(normed, weight):
    flat_field = normed.reshape(normed.shape[0], normed.shape[1] * normed.shape[2])
    result = jnp.dot(jnp.transpose(weight), flat_field, preferred_element_type=jnp.float32)
    return result.reshape(weight.shape[1], normed.shape[1], normed.shape[2])


def contract(first, second, form):
    return jnp.einsum(
        form, first.astype(jnp.float32), second.astype(jnp.float32), precision=lax.Precision.HIGHEST
    )


def body(
    pair_field,
    input_gain,
    input_bias,
    left_weight,
    left_gate,
    right_weight,
    right_gate,
    gate_weight,
    output_gain,
    output_bias,
    final_weight,
):
    gathered = lax.all_gather(pair_field, "ch", axis=0, tiled=True)
    normed = layer_norm(gathered.astype(jnp.float32), input_gain, input_bias).astype(jnp.bfloat16)
    left_factor = (
        jax.nn.sigmoid(project(normed, left_gate)) * project(normed, left_weight)
    ).astype(jnp.bfloat16)
    right_factor = (
        jax.nn.sigmoid(project(normed, right_gate)) * project(normed, right_weight)
    ).astype(jnp.bfloat16)
    gating = jax.nn.sigmoid(project(normed, gate_weight)).astype(jnp.bfloat16)
    product = contract(
        left_factor, lax.all_gather(right_factor, "row", axis=1, tiled=True), "cik,cjk->cij"
    )
    hidden_all = lax.all_gather(product.astype(jnp.bfloat16), "ch", axis=0, tiled=True)
    hidden_normed = layer_norm(hidden_all.astype(jnp.float32), output_gain, output_bias).astype(
        jnp.bfloat16
    )
    update = (gating.astype(jnp.float32) * project(hidden_normed, final_weight)).astype(
        jnp.bfloat16
    )
    return lax.all_to_all(
        jnp.swapaxes(update, 1, 2), "row", split_axis=1, concat_axis=2, tiled=True
    )


def solution(mesh):
    placed = (
        P("ch", "row", None),
        P(),
        P(),
        P(None, "ch"),
        P(None, "ch"),
        P(None, "ch"),
        P(None, "ch"),
        P(None, "ch"),
        P(),
        P(),
        P(None, "ch"),
    )
    return jax.shard_map(
        body, mesh=mesh, in_specs=placed, out_specs=P("ch", "row", None), check_vma=False
    )
```

profile of v0, /device:TPU:1, one launch (start us, length us, event | category | flops | bytes accessed | tf_op | source)
XLA Modules:
  0.0 340.5 jit_solution(7408528371137574967)
XLA Ops:
  6.5 0.0 copy-start
  6.5 0.0 all-gather.4.cloned.1.call-start
  6.5 0.7 all-gather.4.cloned.1.call-update
  7.3 0.0 all-gather.6.cloned.1.call-start
  7.3 29.3 %all-gather.4.cloned.1.call-done = bf16[128,8,512]{2,1,0:T(8,128)(2,1)} async-done(((bf16[32,8,512]{2,1,0:T(8,128)(2,1)}), bf16[128,8,512]{2,1,0:T(8,128)(2,1)}) %all-gather.4.cloned.1.call-update) | async-done | bytes 1048592 | tf_op jit(solution)/shard_map/all_gather | solution.py:41
  36.7 1.5 convert_reduce_fusion.1
  38.2 1.6 fusion.22
  39.7 0.0 copy-done.6
  39.7 0.0 copy-done.7
  39.8 0.0 copy-done.2
  39.8 0.4 fusion.25
  40.2 0.0 copy-start.3
  40.2 0.4 copy.19
  40.6 0.0 copy-done
  40.6 0.0 copy-start.10
  40.6 0.3 fusion.2
  40.9 0.0 copy-done.3
  40.9 0.3 fusion.12
  41.2 0.0 copy-start.4
  41.2 0.8 copy.21
  42.0 0.0 all-gather.6.cloned.1.call-update
  42.0 0.0 all-gather.8.cloned.1.call-start
  42.1 0.0 copy-done.10
  42.1 0.3 fusion.5
  42.4 0.3 fusion.11
  42.7 0.1 copy.20
  42.8 223.6 %all-gather.6.cloned.1.call-done = bf16[32,512,512]{2,1,0:T(8,128)(2,1)} async-done(((bf16[32,8,512]{2,1,0:T(8,128)(2,1)}), bf16[32,512,512]{2,1,0:T(8,128)(2,1)}) %all-gather.6.cloned.1.call-update) | async-done | bytes 16777232 | tf_op jit(solution)/shard_map/all_gather | solution.py:51
  266.4 10.9 %convolution_convert_fusion = bf16[32,8,512]{2,1,0:T(8,128)(2,1)} fusion(bf16[32,8,512]{2,1,0:T(8,128)(2,1)S(1)} %bitcast.48, bf16[32,512,512]{2,1,0:T(8,128)(2,1)} %all-gather.6.cloned.1.call-done), kind=kOutput, calls=%fused_computation.36 | convolution fusion | flops 134348800 | bytes 17301504 | tf_op jit(solution)/shard_map/cik,cjk->cij/dot_general | solution.py:23
  277.3 0.0 all-gather.8.cloned.1.call-update
  277.3 0.0 copy-done.11
  277.3 0.0 copy-start.8
  277.3 0.0 copy-start.9
  277.3 0.3 fusion.10
  277.6 22.2 %all-gather.8.cloned.1.call-done = bf16[128,8,512]{2,1,0:T(8,128)(2,1)} async-done(((bf16[32,8,512]{2,1,0:T(8,128)(2,1)}), bf16[128,8,512]{2,1,0:T(8,128)(2,1)}) %all-gather.8.cloned.1.call-update) | async-done | bytes 1048592 | tf_op jit(solution)/shard_map/all_gather | solution.py:53
  299.9 1.5 convert_reduce_fusion
  301.4 1.6 fusion.18
  303.0 0.0 copy-start.5
  303.0 0.4 fusion.21
  303.4 0.4 copy.22
  303.8 0.3 fusion.13
  304.1 0.1 copy.23
  304.2 0.8 copy.16
  305.1 0.1 bitcast_bitcast_fusion
  305.1 1.0 reshape.87
  306.1 25.8 %all_to_all.18 = bf16[64,2,1024]{2,1,0:T(2,128)(2,1)S(1)} all-to-all(bf16[64,2,1024]{2,1,0:T(2,128)(2,1)S(1)} %reshape.87), channel_id=1, replica_groups=mesh['row'=64,'ch'=4] {'row'}, dimensions={0} | all-to-all | bytes 524288 | tf_op jit(solution)/shard_map/all_to_all | solution.py:60
  332.0 0.5 reshape.88
  332.5 0.2 copy.25
  332.7 1.3 copy.18
  (14 shorter events, 0.1 us)
Async XLA Ops:
  6.5 34.1 %copy-start = (bf16[128,32]{0,1:T(8,128)(2,1)S(1)}, bf16[128,32]{0,1:T(8,128)(2,1)}, u32[]{:S(2)}) copy-start(bf16[128,32]{0,1:T(8,128)(2,1)} %param.17) | copy-start | bytes 24580
  6.5 33.2 %copy-start.6 = (f32[128]{0:T(128)S(1)}, f32[128]{0:T(128)}, u32[]{:S(2)}) copy-start(f32[128]{0:T(128)} %param.13) | copy-start | bytes 1540
  6.5 33.2 %copy-start.7 = (f32[128]{0:T(128)S(1)}, f32[128]{0:T(128)}, u32[]{:S(2)}) copy-start(f32[128]{0:T(128)} %param.12) | copy-start | bytes 1540
  6.5 30.1 %all-gather.4.cloned.1.call-start = ((), (), s32[]{:S(2)}) async-start(), calls=%async_computation.1 | async-start | bytes 1310720 | tf_op jit(solution)/shard_map/all_gather | solution.py:41
  7.3 259.1 %all-gather.6.cloned.1.call-start = ((), (), s32[]{:S(2)}) async-start(), calls=%async_computation.2 | async-start | bytes 17039360 | tf_op jit(solution)/shard_map/all_gather | solution.py:51
  36.7 3.1 copy-start.2
  40.2 0.7 copy-start.3
  40.6 1.5 copy-start.10
  41.2 1.2 copy-start.4
  42.0 257.9 %all-gather.8.cloned.1.call-start = ((), (), s32[]{:S(2)}) async-start(), calls=%async_computation.3 | async-start | bytes 1310720 | tf_op jit(solution)/shard_map/all_gather | solution.py:53
  266.4 11.0 %copy-start.11 = (bf16[128,32]{0,1:T(8,128)(2,1)S(1)}, bf16[128,32]{0,1:T(8,128)(2,1)}, u32[]{:S(2)}) copy-start(bf16[128,32]{0,1:T(8,128)(2,1)} %param.18) | copy-start | bytes 24580
  277.3 25.6 %copy-start.8 = (f32[128]{0:T(128)S(1)}, f32[128]{0:T(128)}, u32[]{:S(2)}) copy-start(f32[128]{0:T(128)} %param.20) | copy-start | bytes 1540
  277.3 25.6 %copy-start.9 = (f32[128]{0:T(128)S(1)}, f32[128]{0:T(128)}, u32[]{:S(2)}) copy-start(f32[128]{0:T(128)} %param.19) | copy-start | bytes 1540
  299.9 3.1 copy-start.1
  303.0 0.8 copy-start.5
Sparse Core Ops, SparseCore 0:
  9.2 27.4 all-gather.3
  42.1 224.1 all-gather.5
  277.4 22.4 all-gather.7
where the time goes:
time: 341 us; the launch traced here: 340 us
  waiting for transfers between devices  276 us (81%)
  blocking collectives  25.8 us (8%)
  between operations  13.4 us (4%)
  matrix products  12.6 us (4%)
  other arithmetic  6.98 us (2%)
  local copies, waits for them, and re-layouts  5.68 us (2%)
    all_gather x1, waiting for transfers between devices, body(): lax.all_gather(right_factor, 'row', axis=1, tiled=True)  224 us
    all_gather x1, waiting for transfers between devices, body(): gathered = lax.all_gather(pair_field, 'ch', axis=0, tiled=True)  29.3 us
    all_to_all x1, blocking collectives, body(): lax.all_to_all(jnp.swapaxes(update, 1, 2), 'row', split_axis=1, concat_ax...  25.8 us
    all_gather x1, waiting for transfers between devices, body(): lax.all_gather(product.astype(jnp.bfloat16), 'ch', axis=0, tiled=True)  22.2 us
    dot_general x1, matrix products, contract(): jnp.einsum(form, first.astype(jnp.float32), second.astype(jnp.float32), p...  10.9 us
  transfers between devices with their start and end apart: 3, of which 3 were waited for; matrix products, arithmetic and copies ran while one was open for 0% of the time, Pallas kernels for 0%

commit v1 on v0

--- a/solution.py
+++ b/solution.py
@@ -4,6 +4,13 @@
 from jax.sharding import PartitionSpec as P
 
 epsilon = 1e-05
+
+
+def draft_kinds_over_axis(local_values, across):
+    e_next = jnp.stack(lax.axis_size(across) * [local_values], axis=0)
+    arr_now = lax.all_to_all(e_next, across, 0, 0)
+    now = jnp.concatenate(arr_now, 1)
+    return now
 
 
 def layer_norm(values, gain, bias):
@@ -47,9 +54,7 @@
         jax.nn.sigmoid(project(normed, right_gate)) * project(normed, right_weight)
     ).astype(jnp.bfloat16)
     gating = jax.nn.sigmoid(project(normed, gate_weight)).astype(jnp.bfloat16)
-    product = contract(
-        left_factor, lax.all_gather(right_factor, "row", axis=1, tiled=True), "cik,cjk->cij"
-    )
+    product = contract(left_factor, draft_kinds_over_axis(right_factor, "row"), "cik,cjk->cij")
     hidden_all = lax.all_gather(product.astype(jnp.bfloat16), "ch", axis=0, tiled=True)
     hidden_normed = layer_norm(hidden_all.astype(jnp.float32), output_gain, output_bias).astype(
         jnp.bfloat16

time: 341 us -> 530 us (1.55)
  waiting for transfers between devices: 276 us -> 448 us
  starting transfers between devices: 0.08 us -> 12.8 us
  local copies, waits for them, and re-layouts: 5.68 us -> 11.3 us
    all_to_all x0 -> x1, waiting for transfers between devices: none -> 377 us  [draft_kinds_over_axis(): arr_now = lax.all_to_all(e_next, across, 0, 0)]
    all_gather x1 -> x0, waiting for transfers between devices: 224 us -> none  [body(): lax.all_gather(right_factor, 'row', axis=1, tiled=True)]
    all_gather x1, waiting for transfers between devices: 22.2 us -> 40.7 us  [body(): lax.all_gather(product.astype(jnp.bfloat16), 'ch', axis=0, tiled=True)]
    all_to_all x0 -> x1, starting transfers between devices: none -> 12.7 us  [draft_kinds_over_axis(): arr_now = lax.all_to_all(e_next, across, 0, 0)]
    another operation x0 -> x1, local copies, waits for them, and re-layouts: none -> 6.02 us  [draft_kinds_over_axis(): e_next = jnp.stack(lax.axis_size(across) * [local_values], axis=0)]
where the time goes in v1:
time: 530 us; the launch traced here: 529 us
  waiting for transfers between devices  448 us (85%)
  blocking collectives  25.8 us (5%)
  between operations  13.7 us (3%)
  starting transfers between devices  12.8 us (2%)
  local copies, waits for them, and re-layouts  11.3 us (2%)
  matrix products  10.5 us (2%)
  other arithmetic  6.98 us (1%)
    all_to_all x1, waiting for transfers between devices, draft_kinds_over_axis(): arr_now = lax.all_to_all(e_next, across, 0, 0)  377 us
    all_gather x1, waiting for transfers between devices, body(): lax.all_gather(product.astype(jnp.bfloat16), 'ch', axis=0, tiled=True)  40.7 us
    all_gather x1, waiting for transfers between devices, body(): gathered = lax.all_gather(pair_field, 'ch', axis=0, tiled=True)  29.4 us
    all_to_all x1, blocking collectives, body(): lax.all_to_all(jnp.swapaxes(update, 1, 2), 'row', split_axis=1, concat_ax...  25.8 us
    all_to_all x1, starting transfers between devices, draft_kinds_over_axis(): arr_now = lax.all_to_all(e_next, across, 0, 0)  12.7 us
  transfers between devices with their start and end apart: 3, of which 3 were waited for; matrix products, arithmetic and copies ran while one was open for 0% of the time, Pallas kernels for 0%

profile of v1, /device:TPU:1, one launch (start us, length us, event | category | flops | bytes accessed | tf_op | source)
XLA Modules:
  0.0 529.3 jit_solution(1450821578878783103)
XLA Ops:
  6.5 0.0 copy-start
  6.5 0.0 all-gather.3.cloned.1.call-start
  6.5 0.7 all-gather.3.cloned.1.call-update
  7.3 29.4 %all-gather.3.cloned.1.call-done = bf16[128,8,512]{2,1,0:T(8,128)(2,1)} async-done(((bf16[32,8,512]{2,1,0:T(8,128)(2,1)}), bf16[128,8,512]{2,1,0:T(8,128)(2,1)}) %all-gather.3.cloned.1.call-update) | async-done | bytes 1048592 | tf_op jit(solution)/shard_map/all_gather | solution.py:48
  36.7 1.5 convert_reduce_fusion.1
  38.2 1.6 fusion.25
  39.7 0.0 copy-done.6
  39.7 0.0 copy-done.7
  39.8 0.0 copy-done.2
  39.8 0.4 fusion.28
  40.2 0.0 copy-start.3
  40.2 0.4 copy.20
  40.6 0.0 copy-done
  40.6 0.3 fusion.5
  40.9 0.0 copy-done.3
  40.9 0.3 fusion.15
  41.2 0.1 copy.22
  41.3 6.0 %stack.2 = bf16[64,32,8,512]{3,2,1,0:T(8,128)(2,1)} broadcast(bf16[32,8,512]{2,1,0:T(8,128)(2,1)S(1)} %bitcast.57), dimensions={1,2,3} | broadcast | bytes 17039360 | tf_op jit(solution)/shard_map/stack | solution.py:10
  47.3 12.7 %all-to-all-start = ((bf16[64,32,8,512]{3,2,1,0:T(8,128)(2,1)}), bf16[64,32,8,512]{3,2,1,0:T(8,128)(2,1)}, u32[]{:S(2)}, u32[]{:S(2)}) async-start(bf16[64,32,8,512]{3,2,1,0:T(8,128)(2,1)} %stack.2), calls=%async_computation | async-start | bytes 33554432 | tf_op jit(solution)/shard_map/all_to_all | solution.py:11
  60.0 0.0 copy-start.4
  60.0 0.0 all-gather.5.cloned.1.call-start
  60.1 0.3 fusion.8
  60.4 0.3 copy-done.4
  60.7 0.3 fusion.14
  61.0 0.1 copy.21
  61.1 377.4 %all-to-all-done = bf16[64,32,8,512]{3,2,1,0:T(8,128)(2,1)} async-done(((bf16[64,32,8,512]{3,2,1,0:T(8,128)(2,1)}), bf16[64,32,8,512]{3,2,1,0:T(8,128)(2,1)}, u32[]{:S(2)}, u32[]{:S(2)}) %all-to-all-start) | async-done | bytes 16777248 | tf_op jit(solution)/shard_map/all_to_all | solution.py:11
  438.5 8.8 %fusion.29 = bf16[32,8,512]{2,1,0:T(8,128)(2,1)} fusion(bf16[32,8,512]{2,1,0:T(8,128)(2,1)S(1)} %bitcast.56, bf16[64,32,8,512]{3,2,1,0:T(8,128)(2,1)} %all-to-all-done), kind=kOutput, calls=%fused_computation.39 | convolution fusion | flops 134348800 | bytes 17301504 | tf_op jit(solution)/shard_map/cik,cjk->cij/dot_general | solution.py:30
  447.3 0.0 all-gather.5.cloned.1.call-update
  447.3 0.0 copy-start.8
  447.4 0.0 copy-start.9
  447.4 0.3 fusion.13
  447.7 40.7 %all-gather.5.cloned.1.call-done = bf16[128,8,512]{2,1,0:T(8,128)(2,1)} async-done(((bf16[32,8,512]{2,1,0:T(8,128)(2,1)}), bf16[128,8,512]{2,1,0:T(8,128)(2,1)}) %all-gather.5.cloned.1.call-update) | async-done | bytes 1048592 | tf_op jit(solution)/shard_map/all_gather | solution.py:58
  488.4 1.5 convert_reduce_fusion
  489.9 1.6 fusion.21
  491.5 0.0 copy-done.8
  491.5 0.0 copy-start.5
  491.5 0.4 fusion.24
  491.9 0.4 copy.23
  492.4 0.0 copy-done.5
  492.4 0.3 fusion.16
  492.6 0.1 copy.24
  492.7 0.8 copy.17
  493.6 0.1 bitcast_bitcast_fusion
  493.7 1.0 reshape.100
  494.7 25.8 %all_to_all.23 = bf16[64,2,1024]{2,1,0:T(2,128)(2,1)S(1)} all-to-all(bf16[64,2,1024]{2,1,0:T(2,128)(2,1)S(1)} %reshape.100), channel_id=1, replica_groups=mesh['row'=64,'ch'=4] {'row'}, dimensions={0} | all-to-all | bytes 524288 | tf_op jit(solution)/shard_map/all_to_all | solution.py:65
  520.5 0.5 reshape.101
  521.0 0.2 copy.32
  521.2 1.3 copy.19
  (14 shorter events, 0.1 us)
Async XLA Ops:
  6.5 34.1 %copy-start = (bf16[128,32]{0,1:T(8,128)(2,1)S(1)}, bf16[128,32]{0,1:T(8,128)(2,1)}, u32[]{:S(2)}) copy-start(bf16[128,32]{0,1:T(8,128)(2,1)} %param.17) | copy-start | bytes 24580
  6.5 33.2 %copy-start.6 = (f32[128]{0:T(128)S(1)}, f32[128]{0:T(128)}, u32[]{:S(2)}) copy-start(f32[128]{0:T(128)} %param.13) | copy-start | bytes 1540
  6.5 33.2 %copy-start.7 = (f32[128]{0:T(128)S(1)}, f32[128]{0:T(128)}, u32[]{:S(2)}) copy-start(f32[128]{0:T(128)} %param.12) | copy-start | bytes 1540
  6.5 30.1 %all-gather.3.cloned.1.call-start = ((), (), s32[]{:S(2)}) async-start(), calls=%async_computation.2 | async-start | bytes 1310720 | tf_op jit(solution)/shard_map/all_gather | solution.py:48
  36.7 3.1 copy-start.2
  40.2 0.7 copy-start.3
  47.3 12.8 %copy-start.10 = (bf16[128,32]{0,1:T(8,128)(2,1)S(1)}, bf16[128,32]{0,1:T(8,128)(2,1)}, u32[]{:S(2)}) copy-start(bf16[128,32]{0,1:T(8,128)(2,1)} %param.15) | copy-start | bytes 24580
  47.3 391.2 %all-to-all-start = ((bf16[64,32,8,512]{3,2,1,0:T(8,128)(2,1)}), bf16[64,32,8,512]{3,2,1,0:T(8,128)(2,1)}, u32[]{:S(2)}, u32[]{:S(2)}) async-start(bf16[64,32,8,512]{3,2,1,0:T(8,128)(2,1)} %stack.2), calls=%async_computation | async-start | bytes 33554432 | tf_op jit(solution)/shard_map/all_to_all | solution.py:11
  60.0 0.7 copy-start.4
  60.0 428.4 %all-gather.5.cloned.1.call-start = ((), (), s32[]{:S(2)}) async-start(), calls=%async_computation.3 | async-start | bytes 1310720 | tf_op jit(solution)/shard_map/all_gather | solution.py:58
  438.5 8.8 %copy-start.11 = (bf16[128,32]{0,1:T(8,128)(2,1)S(1)}, bf16[128,32]{0,1:T(8,128)(2,1)}, u32[]{:S(2)}) copy-start(bf16[128,32]{0,1:T(8,128)(2,1)} %param.18) | copy-start | bytes 24580
  447.3 44.2 %copy-start.8 = (f32[128]{0:T(128)S(1)}, f32[128]{0:T(128)}, u32[]{:S(2)}) copy-start(f32[128]{0:T(128)} %param.20) | copy-start | bytes 1540
  447.4 44.1 %copy-start.9 = (f32[128]{0:T(128)S(1)}, f32[128]{0:T(128)}, u32[]{:S(2)}) copy-start(f32[128]{0:T(128)} %param.19) | copy-start | bytes 1540
  488.4 3.1 copy-start.1
  491.5 0.8 copy-start.5
Sparse Core Ops, SparseCore 0:
  9.2 27.4 all-gather.2
  447.5 40.9 all-gather.4
